TPU v7x, 128 devices: a whole 4x4x4 slice. The times are simulated.
128 devices in a mesh: wave: 32 (over y, x, core), lev: 4 (over z).
Axes of the slice: x: 4, y: 4, z: 4, core: 2. Of those that a mesh axis runs over, the one named last changes fastest.
Arguments:
- legendre: bfloat16 [1280, 1280, 128], P('wave'), may hold values from -0.15625 to 0.15625
- spectral: bfloat16 [1280, 1280, 288], P('wave', None, 'lev'), may hold values from -0.119628906 to 0.119628906
- slot_wave: int32 [1280], P('wave'), may hold values from 0 to 1279, as said below
- band_rows: int32 [256], P(('wave', 'lev')), may hold values from 0 to 255, as said below
- lon_count: int32 [256], P(('wave', 'lev')), may hold values from 20 to 5136, as said below
Outputs:
- grid: float32 [256, 144, 5136], P(('wave', 'lev'))
Inputs may be any that keep to these rules, and one draw needn't show every extreme that they name: slot_wave is a permutation of the wavenumbers; the 40 slots of each index of wave hold 40 consecutive wavenumbers in some order, and which run each index holds is drawn. band_rows is a permutation of the window latitudes. Each northern window latitude has a distance index i from the pole (0 to 1279, indices may repeat), and lon_count[r] = 20 + 4 i for the latitude band_rows[r] mod 128, so a row and its mirror have the same count.
All inputs are finite; a program needn't handle non-finite values.
Results may differ from a plain program's by a relative error of at most 0.0065.
Values sent between devices are 32-bit elements; how exact they have to be, the bound alone decides.
A program may use at most 128 MiB of HBM per device.

v0:
```python
import math

import jax
import jax.numpy as jnp
from jax import lax
from jax.sharding import PartitionSpec as P

TWO_PI = 2.0 * math.pi


def fourier_table_split(waves, number, longs):
    coarse_count = (longs + 63) // 64
    coarse_steps = jnp.arange(coarse_count, dtype=jnp.int32) * 64
    fine_steps = jnp.arange(64, dtype=jnp.int32)
    scale = TWO_PI / number.astype(jnp.float32)
    angle_coarse = (waves[:, None] * coarse_steps[None, :] % number).astype(jnp.float32) * scale
    angle_fine = (waves[:, None] * fine_steps[None, :] % number).astype(jnp.float32) * scale
    cos_coarse = jnp.cos(angle_coarse)[:, :, None]
    sin_coarse = jnp.sin(angle_coarse)[:, :, None]
    cos_fine = jnp.cos(angle_fine)[:, None, :]
    sin_fine = jnp.sin(angle_fine)[:, None, :]
    count = waves.shape[0]
    cosine = (cos_coarse * cos_fine - sin_coarse * sin_fine).reshape(count, coarse_count * 64)[
        :, :longs
    ]
    sine = (sin_coarse * cos_fine + cos_coarse * sin_fine).reshape(count, coarse_count * 64)[
        :, :longs
    ]
    longitude = jnp.arange(longs, dtype=jnp.int32)
    weight = jnp.where(waves == 0, 1.0, 2.0).astype(jnp.float32)
    weight = jnp.where(2 * waves < number, weight, 0.0)
    inside = (longitude < number).astype(jnp.float32)
    cosine = weight[:, None] * cosine * inside[None, :]
    sine = -weight[:, None] * sine * inside[None, :]
    return jnp.stack([cosine, sine], axis=1).astype(jnp.bfloat16)


def on_device(legendre, spectral, slot_wave, band_rows, lon_count):
    slots, depth, north = legendre.shape
    columns = spectral.shape[2]
    all_waves = lax.all_gather(slot_wave, "wave", axis=0, tiled=True)
    all_rows = lax.all_gather(band_rows, ("wave", "lev"), axis=0, tiled=True)
    kblock = math.gcd(depth, 128)
    needed = depth - jnp.min(slot_wave)
    blocks_used = (needed + kblock - 1) // kblock
    zero_value = jnp.zeros((), spectral.dtype)

    def add_block(index, total):
        start = index * kblock
        poles = lax.dynamic_slice_in_dim(legendre, start, kblock, 1)
        coefficient = lax.dynamic_slice_in_dim(spectral, start, kblock, 1)
        depth_index = start + jnp.arange(kblock, dtype=jnp.int32)
        usable = depth_index[None, :] < (depth - slot_wave)[:, None]
        even_mask = usable & (depth_index % 2 == 0)[None, :]
        odd_mask = usable & (depth_index % 2 == 1)[None, :]
        masked = jnp.concatenate(
            [
                jnp.where(even_mask[:, :, None], coefficient, zero_value),
                jnp.where(odd_mask[:, :, None], coefficient, zero_value),
            ],
            axis=2,
        )
        return total + jnp.einsum("skl,skc->slc", poles, masked, preferred_element_type=jnp.float32)

    total = lax.fori_loop(
        0, blocks_used, add_block, jnp.zeros((slots, north, 2 * columns), jnp.float32)
    )
    even_sum = total[:, :, :columns]
    odd_sum = total[:, :, columns:]
    fourier = jnp.concatenate([even_sum + odd_sum, even_sum - odd_sum], axis=1)
    outgoing = jnp.take(fourier, all_rows, axis=1)
    n_wave = lax.axis_size("wave")
    n_lev = lax.axis_size("lev")
    lat_dev = band_rows.shape[0]
    arrived = lax.all_to_all(outgoing, ("wave", "lev"), split_axis=1, concat_axis=0, tiled=True)
    arrived = arrived.reshape(n_wave, n_lev, slots, lat_dev, columns)
    field_dev = columns // 2
    total_waves = all_waves.shape[0]
    arranged = arrived.reshape(n_wave, n_lev, slots, lat_dev, field_dev, 2)
    arranged = arranged.transpose(3, 1, 4, 0, 2, 5).reshape(
        lat_dev, n_lev * field_dev, 2 * total_waves
    )
    longs = 4 * total_waves + 16
    sblock = math.gcd(total_waves, 256)
    nblocks = total_waves // sblock
    outputs = []
    for row in range(lat_dev):
        number = lon_count[row]
        left_row = arranged[row]
        left_high = left_row.astype(jnp.bfloat16)
        left_low = (left_row - left_high.astype(jnp.float32)).astype(jnp.bfloat16)

        def add_part(index, accum):
            start = index * sblock
            waves = lax.dynamic_slice_in_dim(all_waves, start, sblock, 0)
            right = fourier_table_split(waves, number, longs).reshape(2 * sblock, longs)
            part_high = lax.dynamic_slice_in_dim(left_high, 2 * start, 2 * sblock, 1)
            part_low = lax.dynamic_slice_in_dim(left_low, 2 * start, 2 * sblock, 1)
            accum = accum + jnp.dot(part_high, right, preferred_element_type=jnp.float32)
            return accum + jnp.dot(part_low, right, preferred_element_type=jnp.float32)

        outputs.append(
            lax.fori_loop(0, nblocks, add_part, jnp.zeros((n_lev * field_dev, longs), jnp.float32))
        )
    return jnp.stack(outputs, axis=0)


def solution(mesh):
    return jax.shard_map(
        on_device,
        mesh=mesh,
        in_specs=(
            P("wave", None, None),
            P("wave", None, "lev"),
            P("wave"),
            P(("wave", "lev")),
            P(("wave", "lev")),
        ),
        out_specs=P(("wave", "lev"), None, None),
        check_vma=False,
    )
```

profile of v0, /device:TPU:1, one launch (start us, length us, event | category | flops | bytes accessed | tf_op | source)
XLA Modules:
  0.0 716.9 jit_solution(408165682895429199)
XLA Ops:
  2.8 68.7 %all-reduce = s32[256]{0:T(256)S(1)} all-reduce(s32[256]{0:T(256)S(1)} %dynamic-update-slice), channel_id=1, replica_groups=mesh['wave'=32,'lev'=4] {'wave','lev'}, use_global_device_ids=true, to_apply=%add | all-reduce | flops 256 | bytes 2048
  71.7 49.1 %while.44 = (s32[]{:T(128)}, f32[40,128,144]{1,2,0:T(8,128)S(1)}, s32[]{:T(128)}, bf16[40,1280,128]{2,1,0:T(8,128)(2,1)}, s32[40]{0:T(128)}, /*index=5*/bf16[40,...) while((s32[]{:T(128)}, f32[40,128,144]{1,2,0:T(8,128)S(1)}, s32[]{:T(128)}, ...), condition=%wide.region_2.3_spmd, body=%wide.region_1.2_spmd.sunk | while | flops 193184688 | bytes 10918019 | solution.py:65
  131.8 5.7 gather_fusion
  142.0 5.6 all-to-all-start
  153.7 61.4 %all-reduce.1 = s32[1280]{0:T(1024)S(1)} all-reduce(s32[1280]{0:T(1024)S(1)} %dynamic-update-slice.1), channel_id=1, replica_groups=mesh['wave'=32,'lev'=4] {'wave'}, use_global_device_ids=true, to_apply=%add.1 | all-reduce | flops 1280 | bytes 10240
  215.1 8.3 %copy.10 = f32[128,40,2,72]{1,3,2,0:T(8,128)} copy(f32[128,40,2,72]{3,1,2,0:T(8,128)} %bitcast.2) | data formatting | bytes 5898240 | tf_op jit(solution)/shard_map/all_to_all | solution.py:75
  223.4 10.8 %fusion.63 = (f32[1,4,36,32,40,2]{4,5,2,0,1,3:T(2,128)}, f32[1,4,36,32,40,2]{4,5,2,0,1,3:T(2,128)}) fusion(f32[2,4,36,32,40,2]{4,5,2,0,1,3:T(2,128)} %bitcast.59), kind=kLoop, calls=%fused_computation.116 | loop fusion | bytes 5898240 | tf_op jit(solution)/shard_map/slice | solution.py:89
  234.2 9.4 %copy.11 = f32[1,4,36,32,40,2]{2,1,5,4,3,0:T(4,128)} copy(f32[1,4,36,32,40,2]{4,5,2,0,1,3:T(2,128)} %get-tuple-element.591) | data formatting | bytes 2949120 | tf_op jit(solution)/shard_map/slice | solution.py:89
  243.5 5.6 squeeze.12
  258.1 220.8 %while.45 = (s32[]{:T(128)}, f32[144,5136]{1,0:T(8,128)}, bf16[144,2560]{1,0:T(8,128)(2,1)}, s32[1280]{0:T(1024)S(1)}, s32[]{:T(128)}, /*index=5*/s32[]{:T(128)}...) while((s32[]{:T(128)}, f32[144,5136]{1,0:T(8,128)}, ...), condition=%wide.region_4.5_spmd.clone, body=%wide.region_3.4_spmd.clone.sunk | while | flops 1535751040 | bytes 102457408 | solution.py:103
  268.3 13.9 %copy.19 = bf16[256,2,5136]{2,1,0:T(2,128)(2,1)} copy(bf16[256,2,5136]{0,2,1:T(8,128)(2,1)} %pad_maximum_fusion.6) | data formatting | bytes 10518528 | tf_op jit(solution)/shard_map/while/body/eval_jaxpr/stack | solution.py:35
  282.3 11.5 %convert_element_type.239 = bf16[512,5136]{1,0:T(8,128)(2,1)} reshape(bf16[256,2,5136]{2,1,0:T(2,128)(2,1)} %copy.19) | data formatting | bytes 10518528 | tf_op jit(solution)/shard_map/while/body/eval_jaxpr/convert_element_type | solution.py:35
  311.8 13.9 %copy.19 = bf16[256,2,5136]{2,1,0:T(2,128)(2,1)} copy(bf16[256,2,5136]{0,2,1:T(8,128)(2,1)} %pad_maximum_fusion.6) | data formatting | bytes 10518528 | tf_op jit(solution)/shard_map/while/body/eval_jaxpr/stack | solution.py:35
  325.7 11.5 %convert_element_type.239 = bf16[512,5136]{1,0:T(8,128)(2,1)} reshape(bf16[256,2,5136]{2,1,0:T(2,128)(2,1)} %copy.19) | data formatting | bytes 10518528 | tf_op jit(solution)/shard_map/while/body/eval_jaxpr/convert_element_type | solution.py:35
  356.1 13.9 %copy.19 = bf16[256,2,5136]{2,1,0:T(2,128)(2,1)} copy(bf16[256,2,5136]{0,2,1:T(8,128)(2,1)} %pad_maximum_fusion.6) | data formatting | bytes 10518528 | tf_op jit(solution)/shard_map/while/body/eval_jaxpr/stack | solution.py:35
  370.1 11.5 %convert_element_type.239 = bf16[512,5136]{1,0:T(8,128)(2,1)} reshape(bf16[256,2,5136]{2,1,0:T(2,128)(2,1)} %copy.19) | data formatting | bytes 10518528 | tf_op jit(solution)/shard_map/while/body/eval_jaxpr/convert_element_type | solution.py:35
  400.5 13.9 %copy.19 = bf16[256,2,5136]{2,1,0:T(2,128)(2,1)} copy(bf16[256,2,5136]{0,2,1:T(8,128)(2,1)} %pad_maximum_fusion.6) | data formatting | bytes 10518528 | tf_op jit(solution)/shard_map/while/body/eval_jaxpr/stack | solution.py:35
  414.4 11.5 %convert_element_type.239 = bf16[512,5136]{1,0:T(8,128)(2,1)} reshape(bf16[256,2,5136]{2,1,0:T(2,128)(2,1)} %copy.19) | data formatting | bytes 10518528 | tf_op jit(solution)/shard_map/while/body/eval_jaxpr/convert_element_type | solution.py:35
  444.8 13.9 %copy.19 = bf16[256,2,5136]{2,1,0:T(2,128)(2,1)} copy(bf16[256,2,5136]{0,2,1:T(8,128)(2,1)} %pad_maximum_fusion.6) | data formatting | bytes 10518528 | tf_op jit(solution)/shard_map/while/body/eval_jaxpr/stack | solution.py:35
  458.7 11.5 %convert_element_type.239 = bf16[512,5136]{1,0:T(8,128)(2,1)} reshape(bf16[256,2,5136]{2,1,0:T(2,128)(2,1)} %copy.19) | data formatting | bytes 10518528 | tf_op jit(solution)/shard_map/while/body/eval_jaxpr/convert_element_type | solution.py:35
  478.9 9.4 %copy.14 = f32[1,4,36,32,40,2]{2,1,5,4,3,0:T(4,128)} copy(f32[1,4,36,32,40,2]{4,5,2,0,1,3:T(2,128)} %get-tuple-element.592) | data formatting | bytes 2949120 | tf_op jit(solution)/shard_map/slice | solution.py:89
  502.9 209.2 %while.46 = (s32[]{:T(128)}, f32[144,5136]{1,0:T(8,128)S(1)}, bf16[144,2560]{1,0:T(8,128)(2,1)}, s32[1280]{0:T(1024)S(1)}, s32[]{:T(128)}, /*index=5*/s32[]{:T(1...) while((s32[]{:T(128)}, f32[144,5136]{1,0:T(8,128)S(1)}, ...), condition=%wide.region_6.7_spmd.clone, body=%wide.region_5.6_spmd.clone.sunk | while | flops 1535751040 | bytes 102392896 | solution.py:103
  513.0 13.9 %copy.20 = bf16[256,2,5136]{2,1,0:T(2,128)(2,1)} copy(bf16[256,2,5136]{0,2,1:T(8,128)(2,1)} %pad_maximum_fusion.7) | data formatting | bytes 10518528 | tf_op jit(solution)/shard_map/while/body/eval_jaxpr/stack | solution.py:35
  527.0 11.5 %convert_element_type.243 = bf16[512,5136]{1,0:T(8,128)(2,1)} reshape(bf16[256,2,5136]{2,1,0:T(2,128)(2,1)} %copy.20) | data formatting | bytes 10518528 | tf_op jit(solution)/shard_map/while/body/eval_jaxpr/convert_element_type | solution.py:35
  554.9 13.9 %copy.20 = bf16[256,2,5136]{2,1,0:T(2,128)(2,1)} copy(bf16[256,2,5136]{0,2,1:T(8,128)(2,1)} %pad_maximum_fusion.7) | data formatting | bytes 10518528 | tf_op jit(solution)/shard_map/while/body/eval_jaxpr/stack | solution.py:35
  568.8 11.5 %convert_element_type.243 = bf16[512,5136]{1,0:T(8,128)(2,1)} reshape(bf16[256,2,5136]{2,1,0:T(2,128)(2,1)} %copy.20) | data formatting | bytes 10518528 | tf_op jit(solution)/shard_map/while/body/eval_jaxpr/convert_element_type | solution.py:35
  596.7 13.9 %copy.20 = bf16[256,2,5136]{2,1,0:T(2,128)(2,1)} copy(bf16[256,2,5136]{0,2,1:T(8,128)(2,1)} %pad_maximum_fusion.7) | data formatting | bytes 10518528 | tf_op jit(solution)/shard_map/while/body/eval_jaxpr/stack | solution.py:35
  610.6 11.5 %convert_element_type.243 = bf16[512,5136]{1,0:T(8,128)(2,1)} reshape(bf16[256,2,5136]{2,1,0:T(2,128)(2,1)} %copy.20) | data formatting | bytes 10518528 | tf_op jit(solution)/shard_map/while/body/eval_jaxpr/convert_element_type | solution.py:35
  638.5 13.9 %copy.20 = bf16[256,2,5136]{2,1,0:T(2,128)(2,1)} copy(bf16[256,2,5136]{0,2,1:T(8,128)(2,1)} %pad_maximum_fusion.7) | data formatting | bytes 10518528 | tf_op jit(solution)/shard_map/while/body/eval_jaxpr/stack | solution.py:35
  652.5 11.5 %convert_element_type.243 = bf16[512,5136]{1,0:T(8,128)(2,1)} reshape(bf16[256,2,5136]{2,1,0:T(2,128)(2,1)} %copy.20) | data formatting | bytes 10518528 | tf_op jit(solution)/shard_map/while/body/eval_jaxpr/convert_element_type | solution.py:35
  680.4 13.9 %copy.20 = bf16[256,2,5136]{2,1,0:T(2,128)(2,1)} copy(bf16[256,2,5136]{0,2,1:T(8,128)(2,1)} %pad_maximum_fusion.7) | data formatting | bytes 10518528 | tf_op jit(solution)/shard_map/while/body/eval_jaxpr/stack | solution.py:35
  694.3 11.5 %convert_element_type.243 = bf16[512,5136]{1,0:T(8,128)(2,1)} reshape(bf16[256,2,5136]{2,1,0:T(2,128)(2,1)} %copy.20) | data formatting | bytes 10518528 | tf_op jit(solution)/shard_map/while/body/eval_jaxpr/convert_element_type | solution.py:35
  (212 shorter events, 271.3 us)
Async XLA Ops:
  142.0 5.6 copy-start.2
  142.0 9.4 %copy-start.4 = (u32[128]{0:T(128)S(1)}, u32[128]{0:T(128)}, u32[]{:S(2)}) copy-start(u32[128]{0:T(128)} %constant.346) | copy-start | bytes 1540
  142.0 11.4 %copy-start.3 = (s32[40]{0:T(128)S(1)}, s32[40]{0:T(128)}, u32[]{:S(2)}) copy-start(s32[40]{0:T(128)} %get-tuple-element.924) | copy-start | bytes 484
  142.0 73.1 %all-to-all-start = ((f32[40,256,72]{2,0,1:T(8,128)}), f32[40,256,72]{2,0,1:T(8,128)}, u32[]{:S(2)}, u32[]{:S(2)}) async-start(f32[40,256,72]{2,0,1:T(8,128)} %select_bitcast_fusion), calls=%async_computation | async-start | bytes 10485760 | tf_op jit(solution)/shard_map/all_to_all | solution.py:75
  293.8 4.2 copy-start
  337.3 5.0 copy-start
  381.6 5.0 copy-start
  425.9 5.0 copy-start
  470.3 5.0 copy-start
  538.5 4.2 copy-start.1
  580.3 4.2 copy-start.1
  622.2 4.2 copy-start.1
  664.0 4.2 copy-start.1
  705.8 4.2 copy-start.1
where the time goes:
time: 726 us; the launch traced here: 717 us
  local copies, waits for them, and re-layouts  329 us (45%)
  other arithmetic  151 us (21%)
  blocking collectives  130 us (18%)
  matrix products  95 us (13%)
    another operation x10, local copies, waits for them, and re-layouts, fourier_table_split(): return jnp.stack([cosine, sine], axis=1).astype(jnp.bfloat16)  139 us
    unnamed x2, blocking collectives  130 us
    convert_element_type x10, local copies, waits for them, and re-layouts, fourier_table_split(): return jnp.stack([cosine, sine], axis=1).astype(jnp.bfloat16)  115 us
    another operation x20, other arithmetic, fourier_table_split(): return jnp.stack([cosine, sine], axis=1).astype(jnp.bfloat16)  50.2 us
    dot_general x10, matrix products, add_part(): jnp.dot(part_high, right, preferred_element_type=jnp.float32)  41 us
    slice x3, local copies, waits for them, and re-layouts, on_device(): left_row = arranged[row]  29.5 us
    dot_general x10, matrix products, add_part(): return accum + jnp.dot(part_low, right, preferred_element_type=jnp.float32)  28.2 us
    dot_general x10, matrix products, add_block(): jnp.einsum('skl,skc->slc', poles, masked, preferred_element_type=jnp.floa...  25.7 us
  transfers between devices with their start and end apart: 1, of which 0 were waited for; matrix products, arithmetic and copies ran while one was open for 0% of the time, Pallas kernels for 0%

commit v1 on v0

v1 whole, which is shorter than its diff:
```python
import functools
import math

import jax
import jax.numpy as jnp
import numpy as np
from jax import lax
from jax.experimental import pallas as pl
from jax.experimental.pallas import tpu as pltpu
from jax.sharding import PartitionSpec as P

MESH = pl.DeviceIdType.MESH
F32 = jnp.float32
BF16 = jnp.bfloat16

SLOTS = 40
DEPTH = 1280
NORTH = 128
COLS = 72
FIELDS = 144
CHUNKS = 5
TILES = 9
PITCH = 16
PEERS = 128
WIDTH = 1536
RE_ROWS = 576
IM_ROWS = 432
LONS = 5136


def place():
    wave = lax.axis_index("wave")
    return wave // 8, (wave // 2) % 4, wave % 2, lax.axis_index("lev")


def order_of(y, x, core, z):
    return ((core * 4 + z) * 4 + x) * 4 + y


def neighbour(here, offset):
    y = lax.rem(here[0] + offset[0], 4)
    x = lax.rem(here[1] + offset[1], 4)
    core = lax.rem(here[2] + offset[2], 2)
    z = lax.rem(here[3] + offset[3], 4)
    return ((y * 4 + x) * 2 + core, z), order_of(y, x, core, z)


PLANE = [(y, x, 0, 0) for y in range(4) for x in range(4) if y or x]
LINE = [(0, 0, core, z) for core in range(2) for z in range(4) if core or z]


def placement_matrix():
    out = np.zeros((RE_ROWS, 1024), np.float32)
    for row in range(RE_ROWS):
        g, rest = divmod(row, FIELDS)
        z, f = divmod(rest, 36)
        if f < 32:
            out[row, z * 128 + g * 32 + f] = 1.0
        else:
            out[row, 512 + z * 128 + 4 * g + f - 32 : 512 + (z + 1) * 128 : 16] = 1.0
    return out


def quarter_trig(turns):
    near = jnp.floor(turns + 0.5)
    t = turns - near
    t2 = t * t
    h = math.pi / 2
    sine = t * (h + t2 * (-(h**3) / 6 + t2 * (h**5 / 120 + t2 * (-(h**7) / 5040 + t2 * (h**9 / 362880)))))
    cosine = 1.0 + t2 * (-(h**2) / 2 + t2 * (h**4 / 24 + t2 * (-(h**6) / 720 + t2 * (h**8 / 40320))))
    quadrant = near - 4.0 * jnp.floor(near * 0.25)
    odd = (quadrant == 1.0) | (quadrant == 3.0)
    c = jnp.where(odd, sine, cosine)
    s = jnp.where(odd, cosine, sine)
    c = jnp.where((quadrant == 1.0) | (quadrant == 2.0), -c, c)
    s = jnp.where(quadrant >= 2.0, -s, s)
    return c, s


def nt(a, b):
    return lax.dot_general(a, b, (((1,), (1,)), ((), ())), preferred_element_type=F32)


def exchange(
    rows_ref, lon_ref, wave_ref, inv_ref, leg_hbm, spec_hbm, perm_ref, lhs_hbm, tab_hbm,
    leg, spec, left, north, south, entry, hot, sbuf, rbuf, vmat, lhs, tab,
    load_sem, gs_sem, gr_sem, send_sem, recv_sem, own_sem, out_sem, tab_sem,
):
    here = place()
    me = order_of(*here)

    def load(k):
        part = pl.ds(k * 8, 8)
        return (
            pltpu.make_async_copy(leg_hbm.at[part], leg.at[part], load_sem.at[k, 0]),
            pltpu.make_async_copy(spec_hbm.at[part], spec.at[part], load_sem.at[k, 1]),
        )

    for k in range(CHUNKS):
        for copy in load(k):
            copy.start()

    barrier = pltpu.get_barrier_semaphore()
    for offset in PLANE + LINE:
        pl.semaphore_signal(barrier, inc=1, device_id=neighbour(here, offset)[0], device_id_type=MESH)

    lane = lax.broadcasted_iota(jnp.int32, (1, 128), 1)
    mine = jnp.where(lane == 0, rows_ref[0], jnp.where(lane == 1, rows_ref[1], wave_ref[0] // SLOTS))
    entry[pl.ds(me, 1)] = mine.astype(F32).reshape(1, 1, 128)
    left[...] = jnp.zeros_like(left)
    depth_index = lax.broadcasted_iota(jnp.int32, (1, DEPTH), 1)
    sign = jnp.where(depth_index % 2 == 0, 1.0, -1.0)

    def legendre_part(k):
        for copy in load(k):
            copy.wait()

        def one(s, _):
            used = jnp.where(depth_index < DEPTH - wave_ref[s], 1.0, 0.0)
            values = spec[s]
            left[pl.ds(0, COLS), :] = values * used.astype(BF16)
            left[pl.ds(80, COLS), :] = values * (used * sign).astype(BF16)
            sums = jnp.dot(left[...], leg[s], preferred_element_type=F32)
            at = pl.multiple_of(s * COLS, 8)
            north[pl.ds(at, COLS), :] = sums[:COLS]
            south[pl.ds(at, COLS), :] = sums[80 : 80 + COLS]
            return 0

        lax.fori_loop(k * 8, k * 8 + 8, one, 0)

    def gather(offsets, size, first):
        base = (me // size) * size
        copies = []
        for n, offset in enumerate(offsets):
            block = entry.at[pl.ds(base, size)]
            copies.append(
                pltpu.make_async_remote_copy(
                    src_ref=block, dst_ref=block, send_sem=gs_sem.at[first + n], recv_sem=gr_sem.at[first + n],
                    device_id=neighbour(here, offset)[0], device_id_type=MESH,
                )
            )
        return copies

    legendre_part(0)
    legendre_part(1)
    pl.semaphore_wait(barrier, len(PLANE) + len(LINE))
    plane = gather(PLANE, 1, 0)
    for copy in plane:
        copy.start()
    legendre_part(2)
    legendre_part(3)
    for copy in plane:
        copy.wait()
    line = gather(LINE, 16, len(PLANE))
    for copy in line:
        copy.start()
    legendre_part(4)
    for copy in line:
        copy.wait()

    known = entry[...].reshape(PEERS, 128)
    lat = lax.broadcasted_iota(jnp.int32, (PEERS, 256), 1).astype(F32)
    for r in range(2):
        hot[r] = jnp.where(known[:, r : r + 1] == lat, 1.0, 0.0).astype(BF16)
    runs = jnp.concatenate([known[0:16, 2:3], known[64:80, 2:3]], axis=0)

    def send(e, _):
        tails = []
        for c in range(2):
            for u in range(2):
                main, tail = [], []
                for g in range(4):
                    at = inv_ref[(e * 2 + u) * 4 + g] * COLS + c
                    main.append(
                        jnp.concatenate([ref[pl.ds(at, 32, stride=2), :] for ref in (north, south)], axis=1)
                    )
                    tail.append(
                        jnp.concatenate([ref[pl.ds(at + 64, 4, stride=2), :] for ref in (north, south)], axis=1)
                    )
                tails += tail
                main = jnp.concatenate(main, axis=0).astype(BF16)
                for r in range(2):
                    i = r * 4 + c * 2 + u
                    sbuf[pl.ds(e * PEERS * PITCH + i, PEERS, stride=PITCH), :] = nt(hot[r], main)
        tails = jnp.concatenate(tails, axis=0).astype(BF16)
        sbuf[pl.ds(e * PEERS * PITCH + 8, PEERS, stride=PITCH), :] = jnp.concatenate(
            [nt(hot[0], tails), nt(hot[1], tails)], axis=1
        )

        def one(n, _):
            n = lax.rem(n * 53, PEERS)
            device, to = neighbour(here, (n // 32, (n // 8) % 4, (n // 4) % 2, n % 4))
            pltpu.make_async_remote_copy(
                src_ref=sbuf.at[pl.ds((e * PEERS + to) * PITCH, TILES)],
                dst_ref=rbuf.at[pl.ds((e * PEERS + me) * PITCH, TILES)],
                send_sem=send_sem.at[e], recv_sem=recv_sem.at[e], device_id=device, device_id_type=MESH,
            ).start()
            return 0

        lax.fori_loop(1, PEERS, one, 0)
        own = pl.ds((e * PEERS + me) * PITCH, TILES)
        pltpu.make_async_copy(sbuf.at[own], rbuf.at[own], own_sem.at[e]).start()
        return 0

    lax.fori_loop(0, CHUNKS, send, 0)

    column = lax.broadcasted_iota(jnp.int32, (1, 128), 1).astype(F32)

    def fill(n, _):
        r, block = n // (WIDTH // 128), lax.rem(n, WIDTH // 128)
        quarter = (lon_ref[r] // 4).astype(F32)
        inverse = 1.0 / quarter
        p = column + (block * 128).astype(F32)
        at = pl.multiple_of(block * 128, 128)
        for e in range(CHUNKS):
            for u in range(2):
                whole = (runs * 10.0 + (2 * e + u)) * p
                rest = whole - jnp.floor(whole * inverse) * quarter
                c, s = quarter_trig(rest * (4.0 * inverse))
                tab[r, pl.ds(e * 128 + u * 32, 32), pl.ds(at, 128)] = c.astype(BF16)
                tab[r, pl.ds(e * 128 + 64 + u * 32, 32), pl.ds(at, 128)] = s.astype(BF16)
        return 0

    lax.fori_loop(0, 2 * (WIDTH // 128), fill, 0)
    tab_copy = pltpu.make_async_copy(tab, tab_hbm, tab_sem)
    tab_copy.start()

    wide = lax.broadcasted_iota(jnp.int32, (1, 128), 1)
    main_g = (wide // 32).astype(F32)
    tail_g = ((wide % 16) // 4).astype(F32)

    def out_copy(e):
        part = pl.ds(pl.multiple_of(e * 128, 128), 128)
        return pltpu.make_async_copy(lhs.at[:, :, part], lhs_hbm.at[:, :, part], out_sem.at[e])

    def take(e, _):
        total = pl.ds(0, (PEERS - 1) * TILES)
        pltpu.make_async_copy(sbuf.at[total], rbuf.at[total], recv_sem.at[e]).wait()
        own = pl.ds((e * PEERS + me) * PITCH, TILES)
        pltpu.make_async_copy(sbuf.at[own], rbuf.at[own], own_sem.at[e]).wait()

        def rows(core, z, tile):
            return rbuf[pl.ds((e * PEERS + (core * 4 + z) * 16) * PITCH + tile, 16, stride=PITCH), :]

        for r in range(2):
            longs = lon_ref[r].astype(F32)
            for u in range(2):
                m0 = (runs * 10.0 + (2 * e + u).astype(F32)) * 4.0
                m_main, m_tail = m0 + main_g, m0 + tail_g
                weight_main = jnp.where(2.0 * m_main < longs, jnp.where(m_main == 0.0, 1.0, 2.0), 0.0)
                weight_tail = jnp.where(2.0 * m_tail < longs, jnp.where(m_tail == 0.0, 1.0, 2.0), 0.0)
                for c in range(2):
                    i = r * 4 + c * 2 + u
                    picked = jnp.where(wide // 16 == i, weight_tail, 0.0)
                    at = r * 128 + c * 64 + u * 32
                    swapped = r * 128 + (1 - c) * 64 + u * 32
                    for z in range(4):
                        for kind, tile, weight in ((0, i, weight_main), (1, 8, picked)):
                            value = jnp.concatenate([rows(0, z, tile), rows(1, z, tile)], axis=0) * weight
                            lanes = pl.ds((kind * 4 + z) * 128, 128)
                            vmat[0, pl.ds(at, 32), lanes] = (value if c == 0 else -value).astype(BF16)
                            vmat[1, pl.ds(swapped, 32), lanes] = value.astype(BF16)
        part = pl.ds(pl.multiple_of(e * 128, 128), 128)
        real = nt(perm_ref[...], vmat[0]).astype(BF16)
        imag = nt(perm_ref[pl.ds(FIELDS, IM_ROWS), :], vmat[1]).astype(BF16)
        for r in range(2):
            lhs[r, pl.ds(0, RE_ROWS), part] = real[:, r * 128 : (r + 1) * 128]
            lhs[r, pl.ds(RE_ROWS, IM_ROWS), part] = imag[:, r * 128 : (r + 1) * 128]
        out_copy(e).start()
        return 0

    lax.fori_loop(0, CHUNKS, take, 0)

    def finish(e, _):
        total = pl.ds(0, (PEERS - 1) * TILES)
        pltpu.make_async_copy(sbuf.at[total], rbuf.at[total], send_sem.at[e]).wait()
        out_copy(e).wait()
        return 0

    lax.fori_loop(0, CHUNKS, finish, 0)
    tab_copy.wait()


def synthesis(lon_ref, lhs_ref, tab_ref, out_ref, zbuf, parts, line):
    r = pl.program_id(0)
    longs = lon_ref[r]
    quarter = longs // 4
    scale = 4.0 / longs.astype(F32)
    parts[...] = jnp.zeros_like(parts)

    def block(n, _):
        at = pl.multiple_of(n * 256, 256)
        zbuf[...] = jnp.dot(lhs_ref[0], tab_ref[0, :, pl.ds(at, 256)], preferred_element_type=F32)
        p = lax.broadcasted_iota(jnp.int32, (8, 256), 1) + at
        inside = jnp.where(p < quarter, 1.0, 0.0)
        pf = p.astype(F32)
        c1, s1 = quarter_trig(pf * scale)
        c2, s2 = quarter_trig(2.0 * pf * scale)
        c3, s3 = quarter_trig(3.0 * pf * scale)
        c1, s1, c2, s2, c3, s3 = (v * inside for v in (c1, s1, c2, s2, c3, s3))

        def rows(b, _):
            def get(row):
                return zbuf[pl.ds(pl.multiple_of(row + b * 8, 8), 8), :]

            re0, re1, re2, re3 = (get(g * FIELDS) for g in range(4))
            im1, im2, im3 = (get(RE_ROWS + g * FIELDS) for g in range(3))
            a0 = re0 * inside
            a2 = c2 * re2 - s2 * im2
            r1, i1 = c1 * re1 - s1 * im1, c1 * im1 + s1 * re1
            r3, i3 = c3 * re3 - s3 * im3, c3 * im3 + s3 * re3
            plus, minus = a0 + a2, a0 - a2
            across, along = r1 + r3, i1 - i3
            at_rows = pl.ds(pl.multiple_of(b * 8, 8), 8)
            for t, value in enumerate((plus + across, minus - along, plus - across, minus + along)):
                parts[t, at_rows, pl.ds(at, 256)] = value
            return 0

        lax.fori_loop(0, FIELDS // 8, rows, 0)
        return 0

    lax.fori_loop(0, WIDTH // 256, block, 0)

    def place_rows(b, _):
        at_rows = pl.ds(pl.multiple_of(b * 8, 8), 8)
        line[...] = jnp.zeros_like(line)
        for t in range(4):
            start = t * quarter
            moved = pltpu.roll(parts[t, at_rows, :], lax.rem(start, 128), axis=1)
            lanes = pl.ds(pl.multiple_of((start // 128) * 128, 128), WIDTH + 128)
            line[:, lanes] = line[:, lanes] + moved
        out_ref[0, at_rows, :] = line[:, :LONS]
        return 0

    lax.fori_loop(0, FIELDS // 8, place_rows, 0)


def on_device(legendre, spectral, slot_wave, band_rows, lon_count):
    slot = jnp.arange(SLOTS, dtype=jnp.int32)
    within = slot_wave % SLOTS
    inverse = jnp.sum(jnp.where(within[None, :] == slot[:, None], slot[None, :], 0), axis=1)
    perm = jnp.asarray(placement_matrix(), BF16)
    anywhere = pl.BlockSpec(memory_space=pl.ANY)
    smem = pl.BlockSpec(memory_space=pltpu.SMEM)
    dma = pltpu.SemaphoreType.DMA
    n_gather = len(PLANE) + len(LINE)
    lhs, tab = pl.pallas_call(
        exchange,
        out_shape=(
            jax.ShapeDtypeStruct((2, RE_ROWS + IM_ROWS, 640), BF16),
            jax.ShapeDtypeStruct((2, 640, WIDTH), BF16),
        ),
        in_specs=[smem, smem, smem, smem, anywhere, anywhere, pl.BlockSpec(memory_space=pltpu.VMEM)],
        out_specs=(anywhere, anywhere),
        scratch_shapes=[
            pltpu.VMEM((SLOTS, DEPTH, NORTH), BF16),
            pltpu.VMEM((SLOTS, COLS, DEPTH), BF16),
            pltpu.VMEM((160, DEPTH), BF16),
            pltpu.VMEM((SLOTS * COLS, 128), F32),
            pltpu.VMEM((SLOTS * COLS, 128), F32),
            pltpu.VMEM((PEERS, 1, 128), F32),
            pltpu.VMEM((2, PEERS, 256), BF16),
            pltpu.VMEM((CHUNKS * PEERS * PITCH, 128), F32),
            pltpu.VMEM((CHUNKS * PEERS * PITCH, 128), F32),
            pltpu.VMEM((2, 256, 1024), BF16),
            pltpu.VMEM((2, RE_ROWS + IM_ROWS, 640), BF16),
            pltpu.VMEM((2, 640, WIDTH), BF16),
            dma((CHUNKS, 2)),
            dma((n_gather,)),
            dma((n_gather,)),
            dma((CHUNKS,)),
            dma((CHUNKS,)),
            dma((CHUNKS,)),
            dma((CHUNKS,)),
            dma,
        ],
        compiler_params=pltpu.CompilerParams(collective_id=0, has_side_effects=True, vmem_limit_bytes=58 << 20),
    )(band_rows, lon_count, slot_wave, inverse, legendre, jnp.swapaxes(spectral, 1, 2), perm)
    return pl.pallas_call(
        synthesis,
        grid_spec=pltpu.PrefetchScalarGridSpec(
            num_scalar_prefetch=1,
            grid=(2,),
            in_specs=[
                pl.BlockSpec((1, RE_ROWS + IM_ROWS, 640), lambda r, _: (r, 0, 0)),
                pl.BlockSpec((1, 640, WIDTH), lambda r, _: (r, 0, 0)),
            ],
            out_specs=pl.BlockSpec((1, FIELDS, LONS), lambda r, _: (r, 0, 0)),
            scratch_shapes=[
                pltpu.VMEM((RE_ROWS + IM_ROWS, 256), F32),
                pltpu.VMEM((4, FIELDS, WIDTH + 128), F32),
                pltpu.VMEM((8, 5504), F32),
            ],
        ),
        out_shape=jax.ShapeDtypeStruct((2, FIELDS, LONS), F32),
        compiler_params=pltpu.CompilerParams(vmem_limit_bytes=58 << 20),
    )(lon_count, lhs, tab)


def solution(mesh):
    return jax.shard_map(
        on_device,
        mesh=mesh,
        in_specs=(
            P("wave", None, None),
            P("wave", None, "lev"),
            P("wave"),
            P(("wave", "lev")),
            P(("wave", "lev")),
        ),
        out_specs=P(("wave", "lev"), None, None),
        check_vma=False,
    )
```

time: 726 us -> 85.1 us (0.12); the launches traced: 717 us -> 84.9 us
  local copies, waits for them, and re-layouts: 329 us -> 0 us
  other arithmetic: 151 us -> 1.29 us
  blocking collectives: 130 us -> 0 us
  matrix products: 95 us -> 0 us
  Pallas kernels: 0 us -> 83.6 us
    another operation x10 -> x0, local copies, waits for them, and re-layouts: 139 us -> none  [fourier_table_split(): return jnp.stack([cosine, sine], axis=1).astype(jnp.bfloat16)]
    unnamed x2 -> x0, blocking collectives: 130 us -> none
    convert_element_type x10 -> x0, local copies, waits for them, and re-layouts: 115 us -> none  [fourier_table_split(): return jnp.stack([cosine, sine], axis=1).astype(jnp.bfloat16)]
    dot_general x30 -> x0, matrix products: 95 us -> none  [the longest x10 41 us: add_part(): jnp.dot(part_high, right, preferred_element_type=jnp.float32)]
    pallas_call x0 -> x2, Pallas kernels: none -> 83.6 us  [the longest x1 63.5 us: on_device(): pl.pallas_call(exchange, out_shape=(jax.ShapeDtypeStruct((2, RE_ROWS + IM...]
    another operation x21 -> x0, other arithmetic: 55.1 us -> none  [the longest x20 50.2 us: fourier_table_split(): return jnp.stack([cosine, sine], axis=1).astype(jnp.bfloat16)]
    slice x4 -> x0, local copies, waits for them, and re-layouts: 30.1 us -> none  [the longest x3 29.5 us: on_device(): left_row = arranged[row]]
    cos x20 -> x0, other arithmetic: 22.2 us -> none  [the longest x10 13 us: fourier_table_split(): cos_coarse = jnp.cos(angle_coarse)[:, :, None]]
  transfers between devices with their start and end apart: 1 -> 0, of which waited for: 0 -> 0; matrix products, arithmetic and copies ran while one was open for 0% -> 0% of each run, Pallas kernels for 0% -> 0%
where the time goes in v1:
time: 85.1 us; the launch traced here: 84.9 us
  Pallas kernels  83.6 us (98%)
  other arithmetic  1.29 us (2%)
    pallas_call x1, Pallas kernels, on_device(): pl.pallas_call(exchange, out_shape=(jax.ShapeDtypeStruct((2, RE_ROWS + IM...  63.5 us
    pallas_call x1, Pallas kernels, on_device(): pl.pallas_call(synthesis, grid_spec=pltpu.PrefetchScalarGridSpec(num_scal...  20.1 us

profile of v1, /device:TPU:1, one launch (start us, length us, event | category | flops | bytes accessed | tf_op | source)
XLA Modules:
  0.0 84.9 jit_solution(278437451006459971)
XLA Ops:
  0.0 0.7 and_select_fusion
  0.7 0.6 select_reduce_fusion.inv_ref
  1.3 63.5 %shard_map.64 = (bf16[2,1008,640]{2,1,0:T(8,128)(2,1)}, bf16[2,640,1536]{2,1,0:T(8,128)(2,1)}) custom-call(s32[2]{0:T(128)} %rows_ref.1, s32[2]{0:T(128)} %lon_ref.3, s32[40]{0:T(128)} %wave_ref.1, s32[40]{0:T(128)} %select_reduce_fusion.inv_ref, bf16[40,1280,128]{2,1,0:T(8,128)(2,1)} %leg_hbm.1, bf16[40,72,1280]{2,1,0:T(8,128)(2,1)} %bitcast.1, ...), custom_call_target="tpu_custom_call" | custom-call | tf_op jit(solution)/shard_map/pallas_call | solution.py:347
  64.8 20.1 %shard_map.65 = f32[2,144,5136]{2,1,0:T(8,128)} custom-call(s32[2]{0:T(128)} %lon_ref.3, bf16[2,1008,640]{2,1,0:T(8,128)(2,1)} %get-tuple-element.7.lhs_ref, bf16[2,640,1536]{2,1,0:T(8,128)(2,1)} %get-tuple-element.8.tab_ref), custom_call_target="tpu_custom_call" | custom-call | tf_op jit(solution)/shard_map/pallas_call | solution.py:379

commit v2 on v1

v2 whole, which is shorter than its diff:
```python
import functools
import math

import jax
import jax.numpy as jnp
import numpy as np
from jax import lax
from jax.experimental import pallas as pl
from jax.experimental.pallas import tpu as pltpu
from jax.sharding import PartitionSpec as P

MESH = pl.DeviceIdType.MESH
F32 = jnp.float32
BF16 = jnp.bfloat16

SLOTS = 40
DEPTH = 1280
NORTH = 128
COLS = 72
FIELDS = 144
CHUNKS = 5
TILES = 9
GROUPS = (2, 2, 1)
PITCH = 24
PEERS = 128
WIDTH = 1408
HALF = 72
RE_ROWS = 4 * HALF
IM_ROWS = 3 * HALF
ROWS = RE_ROWS + IM_ROWS
TURNS = 56
LONS = 5136


def place():
    wave = lax.axis_index("wave")
    return wave // 8, (wave // 2) % 4, wave % 2, lax.axis_index("lev")


def order_of(y, x, core, z):
    return ((core * 4 + z) * 4 + x) * 4 + y


def neighbour(here, offset):
    y = lax.rem(here[0] + offset[0], 4)
    x = lax.rem(here[1] + offset[1], 4)
    core = lax.rem(here[2] + offset[2], 2)
    z = lax.rem(here[3] + offset[3], 4)
    return ((y * 4 + x) * 2 + core, z), order_of(y, x, core, z)


PLANE = [(y, x, 0, 0) for y in range(4) for x in range(4) if y or x]
LINE_PLACES = [(1, 0), (0, 1), (1, 2), (0, 3), (1, 1), (0, 2), (1, 3)]
LINE = [(0, 0, core, z) for core in range(2) for z in range(4) if core or z]


def placement_matrix():
    out = np.zeros((2, 4, HALF, 1024), np.float32)
    for half in range(2):
        for g in range(4):
            for f in range(HALF):
                z, k = divmod(half * HALF + f, 36)
                if k < 32:
                    out[half, g, f, z * 128 + g * 32 + k] = 1.0
                else:
                    out[half, g, f, 512 + z * 128 + 4 * g + k - 32 : 512 + (z + 1) * 128 : 16] = 1.0
    return out.reshape(2, RE_ROWS, 1024)


def quarter_trig(turns):
    near = jnp.floor(turns + 0.5)
    t = turns - near
    t2 = t * t
    h = math.pi / 2
    sine = t * (h + t2 * (-(h**3) / 6 + t2 * (h**5 / 120 + t2 * (-(h**7) / 5040 + t2 * (h**9 / 362880)))))
    cosine = 1.0 + t2 * (-(h**2) / 2 + t2 * (h**4 / 24 + t2 * (-(h**6) / 720 + t2 * (h**8 / 40320))))
    quadrant = near - 4.0 * jnp.floor(near * 0.25)
    odd = (quadrant == 1.0) | (quadrant == 3.0)
    c = jnp.where(odd, sine, cosine)
    s = jnp.where(odd, cosine, sine)
    c = jnp.where((quadrant == 1.0) | (quadrant == 2.0), -c, c)
    s = jnp.where(quadrant >= 2.0, -s, s)
    return c, s


def nt(a, b):
    return lax.dot_general(a, b, (((1,), (1,)), ((), ())), preferred_element_type=F32)


def exchange(
    rows_ref, lon_ref, wave_ref, leg_hbm, spec_hbm, perm_hbm, lhs_hbm, tab_hbm, turn_hbm,
    leg, spec, perm, left, north, south, entry, inv_vmem, inv_ref, hot, sbuf, rbuf, vmat, lhs, tab, turn,
    load_sem, perm_sem, inv_sem, gs_sem, gr_sem, send_sem, recv_sem, own_sem, out_sem, tab_sem, turn_sem,
):
    here = place()
    me = order_of(*here)

    def load(k):
        part = pl.ds(k * 8, 8)
        return (
            pltpu.make_async_copy(leg_hbm.at[part], leg.at[part], load_sem.at[k, 0]),
            pltpu.make_async_copy(spec_hbm.at[part], spec.at[part], load_sem.at[k, 1]),
        )

    for k in range(CHUNKS):
        for copy in load(k):
            copy.start()

    perm_copy = pltpu.make_async_copy(perm_hbm, perm, perm_sem)
    perm_copy.start()

    barrier = pltpu.get_barrier_semaphore()
    for offset in PLANE + LINE:
        pl.semaphore_signal(barrier, inc=1, device_id=neighbour(here, offset)[0], device_id_type=MESH)

    lane = lax.broadcasted_iota(jnp.int32, (1, 128), 1)
    mine = jnp.where(lane == 0, rows_ref[0], jnp.where(lane == 1, rows_ref[1], wave_ref[0] // SLOTS))
    entry[pl.ds(me, 1)] = mine.astype(F32).reshape(1, 1, 128)
    left[...] = jnp.zeros_like(left)

    within = jnp.full((1, 128), SLOTS, jnp.int32)
    for s in range(SLOTS):
        within = jnp.where(lane == s, lax.rem(wave_ref[s], SLOTS), within)
    wanted = lax.broadcasted_iota(jnp.int32, (SLOTS, 128), 0)
    slot = lax.broadcasted_iota(jnp.int32, (SLOTS, 128), 1)
    found = jnp.max(jnp.where(within == wanted, slot, 0), axis=1, keepdims=True)
    inv_vmem[...] = jnp.broadcast_to(found, (SLOTS, 128))
    inv_copy = pltpu.make_async_copy(inv_vmem, inv_ref, inv_sem)
    inv_copy.start()
    depth_index = lax.broadcasted_iota(jnp.int32, (1, DEPTH), 1)
    sign = jnp.where(depth_index % 2 == 0, 1.0, -1.0)

    def legendre_part(k):
        for copy in load(k):
            copy.wait()

        def four(n, _):
            for q in range(4):
                s = k * 8 + n * 4 + q
                used = jnp.where(depth_index < DEPTH - wave_ref[s], 1.0, 0.0)
                values = spec[s]
                left[q, pl.ds(0, COLS), :] = values * used.astype(BF16)
                left[q, pl.ds(80, COLS), :] = values * (used * sign).astype(BF16)
                sums = jnp.dot(left[q], leg[s], preferred_element_type=F32)
                at = pl.multiple_of(s * COLS, 8)
                north[pl.ds(at, COLS), :] = sums[:COLS]
                south[pl.ds(at, COLS), :] = sums[80 : 80 + COLS]
            return 0

        lax.fori_loop(0, 2, four, 0)

    def gather(offsets, size, first):
        base = (me // size) * size
        copies = []
        for n, offset in enumerate(offsets):
            block = entry.at[pl.ds(base, size)]
            copies.append(
                pltpu.make_async_remote_copy(
                    src_ref=block, dst_ref=block, send_sem=gs_sem.at[first + n], recv_sem=gr_sem.at[first + n],
                    device_id=neighbour(here, offset)[0], device_id_type=MESH,
                )
            )
        return copies

    legendre_part(0)
    legendre_part(1)
    pl.semaphore_wait(barrier, len(PLANE) + len(LINE))
    plane = gather(PLANE, 1, 0)
    for copy in plane:
        copy.start()
    legendre_part(2)
    legendre_part(3)
    for copy in plane:
        copy.wait()
    line = gather(LINE, 16, len(PLANE))
    for copy in line:
        copy.start()
    legendre_part(4)
    for copy in line:
        copy.wait()

    inv_copy.wait()
    perm_copy.wait()
    known = entry[...].reshape(PEERS, 128)
    lat = lax.broadcasted_iota(jnp.int32, (PEERS, 256), 1).astype(F32)
    for r in range(2):
        hot[r] = jnp.where(known[:, r : r + 1] == lat, 1.0, 0.0).astype(BF16)
    runs = jnp.concatenate([known[0:16, 2:3], known[64:80, 2:3]], axis=0)

    def first_row(e):
        return (e // 2) * PEERS * PITCH + (e % 2) * TILES

    def pack(e, _):
        tails = []
        for c in range(2):
            for u in range(2):
                main, tail = [], []
                for g in range(4):
                    at = inv_ref[(e * 2 + u) * 4 + g, 0] * COLS + c
                    main.append(
                        jnp.concatenate([ref[pl.ds(at, 32, stride=2), :] for ref in (north, south)], axis=1)
                    )
                    tail.append(
                        jnp.concatenate([ref[pl.ds(at + 64, 4, stride=2), :] for ref in (north, south)], axis=1)
                    )
                tails += tail
                main = jnp.concatenate(main, axis=0).astype(BF16)
                for r in range(2):
                    i = r * 4 + c * 2 + u
                    sbuf[pl.ds(first_row(e) + i, PEERS, stride=PITCH), :] = nt(hot[r], main)
        tails = jnp.concatenate(tails, axis=0).astype(BF16)
        sbuf[pl.ds(first_row(e) + 8, PEERS, stride=PITCH), :] = jnp.concatenate(
            [nt(hot[0], tails), nt(hot[1], tails)], axis=1
        )

        return 0

    def own_copy(k):
        own = pl.ds((k * PEERS + me) * PITCH, GROUPS[k] * TILES)
        return pltpu.make_async_copy(sbuf.at[own], rbuf.at[own], own_sem.at[k])

    def send(k, n, skip):
        for j, (core, z) in enumerate([(0, 0)] + LINE_PLACES):
            if j == skip:
                continue
            xy = lax.rem(n * 5 + j * 7, 16)
            device, to = neighbour(here, (xy // 4, lax.rem(xy, 4), core, z))
            size = GROUPS[k] * TILES
            pltpu.make_async_remote_copy(
                src_ref=sbuf.at[pl.ds((k * PEERS + to) * PITCH, size)],
                dst_ref=rbuf.at[pl.ds((k * PEERS + me) * PITCH, size)],
                send_sem=send_sem.at[k], recv_sem=recv_sem.at[k], device_id=device, device_id_type=MESH,
            ).start()

    column = lax.broadcasted_iota(jnp.int32, (1, 128), 1).astype(F32)

    def fill(n, _):
        r, block = n // (WIDTH // 128), lax.rem(n, WIDTH // 128)
        quarter = (lon_ref[r] // 4).astype(F32)
        inverse = 1.0 / quarter
        p = column + (block * 128).astype(F32)
        at = pl.multiple_of(block * 128, 128)
        for e in range(CHUNKS):
            for u in range(2):
                whole = (runs * 10.0 + (2 * e + u)) * p
                rest = whole - jnp.floor(whole * inverse) * quarter
                c, s = quarter_trig(rest * (4.0 * inverse))
                tab[r, pl.ds(e * 128 + u * 32, 32), pl.ds(at, 128)] = c.astype(BF16)
                tab[r, pl.ds(e * 128 + 64 + u * 32, 32), pl.ds(at, 128)] = s.astype(BF16)
        step = 4.0 / lon_ref[r].astype(F32)
        inside = jnp.where(p < quarter, 1.0, 0.0)
        kept = [inside]
        for g in range(1, 4):
            kept += quarter_trig(p * (g * step))
        for k, value in enumerate(kept):
            turn[r, pl.ds(k * 8, 8), pl.ds(at, 128)] = jnp.broadcast_to(value * inside, (8, 128))
        return 0

    tab_copy = pltpu.make_async_copy(tab, tab_hbm, tab_sem)
    turn_copy = pltpu.make_async_copy(turn, turn_hbm, turn_sem)

    wide = lax.broadcasted_iota(jnp.int32, (1, 128), 1)
    main_g = (wide // 32).astype(F32)
    tail_g = ((wide % 16) // 4).astype(F32)

    def out_copy(e):
        part = pl.ds(pl.multiple_of(e * 128, 128), 128)
        return pltpu.make_async_copy(lhs.at[:, :, part], lhs_hbm.at[:, :, part], out_sem.at[e])

    def take(e, _):
        def rows(core, z, tile):
            return rbuf[pl.ds(first_row(e) + (core * 4 + z) * 16 * PITCH + tile, 16, stride=PITCH), :]

        for r in range(2):
            longs = lon_ref[r].astype(F32)
            for u in range(2):
                m0 = (runs * 10.0 + (2 * e + u).astype(F32)) * 4.0
                m_main, m_tail = m0 + main_g, m0 + tail_g
                weight_main = jnp.where(2.0 * m_main < longs, jnp.where(m_main == 0.0, 1.0, 2.0), 0.0)
                weight_tail = jnp.where(2.0 * m_tail < longs, jnp.where(m_tail == 0.0, 1.0, 2.0), 0.0)
                for c in range(2):
                    i = r * 4 + c * 2 + u
                    picked = jnp.where(wide // 16 == i, weight_tail, 0.0)
                    at = r * 128 + c * 64 + u * 32
                    swapped = r * 128 + (1 - c) * 64 + u * 32
                    for z in range(4):
                        for kind, tile, weight in ((0, i, weight_main), (1, 8, picked)):
                            value = jnp.concatenate([rows(0, z, tile), rows(1, z, tile)], axis=0) * weight
                            lanes = pl.ds((kind * 4 + z) * 128, 128)
                            vmat[0, pl.ds(at, 32), lanes] = (value if c == 0 else -value).astype(BF16)
                            vmat[1, pl.ds(swapped, 32), lanes] = value.astype(BF16)
        part = pl.ds(pl.multiple_of(e * 128, 128), 128)
        for half in range(2):
            real = nt(perm[half], vmat[0]).astype(BF16)
            imag = nt(perm[half, pl.ds(HALF, IM_ROWS), :], vmat[1]).astype(BF16)
            for r in range(2):
                lhs[r * 2 + half, pl.ds(0, RE_ROWS), part] = real[:, r * 128 : (r + 1) * 128]
                lhs[r * 2 + half, pl.ds(RE_ROWS, IM_ROWS), part] = imag[:, r * 128 : (r + 1) * 128]
        out_copy(e).start()
        return 0

    def whole(k, sem):
        total = pl.ds(0, (PEERS - 1) * GROUPS[k] * TILES)
        return pltpu.make_async_copy(sbuf.at[total], rbuf.at[total], sem.at[k])

    blocks = 2 * (WIDTH // 128)
    done = 0
    for k in range(3):
        lax.fori_loop(2 * k, 2 * k + GROUPS[k], pack, 0)
        own_copy(k).start()
        send(k, 0, 0)
        filled = min(done + 15, blocks)

        def some(n, _):
            send(k, n, -1)
            fill(done + n - 1, 0)
            return 0

        def rest(n, _):
            send(k, n, -1)
            return 0

        lax.fori_loop(1, 1 + filled - done, some, 0)
        lax.fori_loop(1 + filled - done, 16, rest, 0)
        done = filled
    tab_copy.start()
    turn_copy.start()
    for k in range(3):
        whole(k, recv_sem).wait()
        own_copy(k).wait()
        lax.fori_loop(2 * k, 2 * k + GROUPS[k], take, 0)
    for k in range(3):
        whole(k, send_sem).wait()
    for e in range(CHUNKS):
        out_copy(e).wait()
    tab_copy.wait()
    turn_copy.wait()


def synthesis(
    lon_ref, lhs_hbm, tab_hbm, turn_hbm, out_hbm,
    lhs, tab, turn, z0, z1, parts0, parts1, out0, out1, lhs_sem, tab_sem, turn_sem, out_sem,
):
    sums, outs = (z0, z1), (out0, out1)

    def lhs_copy(s):
        return pltpu.make_async_copy(lhs_hbm.at[s], lhs.at[s], lhs_sem.at[s])

    def tab_copy(r):
        return pltpu.make_async_copy(tab_hbm.at[r], tab.at[r], tab_sem.at[r])

    def turn_copy(r):
        return pltpu.make_async_copy(turn_hbm.at[r], turn.at[r], turn_sem.at[r])

    def out_copy(s):
        rows = out_hbm.at[s // 2, pl.ds((s % 2) * HALF, HALF), :]
        return pltpu.make_async_copy(outs[s % 2], rows, out_sem.at[s % 2])

    tab_copy(0).start()
    lhs_copy(0).start()
    turn_copy(0).start()
    lhs_copy(1).start()
    tab_copy(1).start()
    turn_copy(1).start()
    lhs_copy(2).start()
    lhs_copy(3).start()
    for ref in sums:
        ref[:, WIDTH - 128 :] = jnp.zeros((ROWS, 128), F32)
    lane = lax.broadcasted_iota(jnp.int32, (8, 128), 1)

    def product(s, at, width):
        sums[s % 2][:, pl.ds(at, width)] = jnp.dot(
            lhs[s], tab[s // 2, :, pl.ds(at, width)], preferred_element_type=F32
        )

    def unit(s, b, parts):
        source, out, r = sums[s % 2], outs[s % 2], s // 2
        quarter = lon_ref[r] // 4
        rows = pl.ds(pl.multiple_of(b * 8, 8), 8)
        for j in range(WIDTH // 128):
            lanes = pl.ds(j * 128, 128)

            def get(row):
                return source[pl.ds(pl.multiple_of(row * HALF + b * 8, 8), 8), lanes]

            re0, re1, re2, re3, im1, im2, im3 = (get(k) for k in range(7))
            inside, c1, s1, c2, s2, c3, s3 = (turn[r, pl.ds(k * 8, 8), lanes] for k in range(7))
            a0 = re0 * inside
            a2 = c2 * re2 - s2 * im2
            r1, i1 = c1 * re1 - s1 * im1, c1 * im1 + s1 * re1
            r3, i3 = c3 * re3 - s3 * im3, c3 * im3 + s3 * re3
            plus, minus = a0 + a2, a0 - a2
            across, along = r1 + r3, i1 - i3
            for t, value in enumerate((plus + across, minus - along, plus - across, minus + along)):
                parts[pl.ds(t * 8, 8), lanes] = value
        for t in range(4):
            start = t * quarter
            first, shift = start // 128, lax.rem(start, 128)
            below = lane < shift
            before = out[rows, pl.ds(pl.multiple_of(first * 128, 128), 128)]
            previous = None
            for j in range(WIDTH // 128):
                turned = pltpu.roll(parts[pl.ds(t * 8, 8), pl.ds(j * 128, 128)], shift, axis=1)
                value = jnp.where(below, before, turned)
                before = turned
                if t == 3 and j == WIDTH // 128 - 1:
                    full = first == 30
                    out[rows, pl.ds(5120, 16)] = jnp.where(full, value, 0.0)[:, :16]
                    value = jnp.where(full, previous, value)
                    place_at = jnp.minimum(first + j, 39)
                else:
                    place_at = first + j
                out[rows, pl.ds(pl.multiple_of(place_at * 128, 128), 128)] = value
                previous = value

    for s in range(5):
        if s < 4:
            lhs_copy(s).wait()
            if s % 2 == 0:
                tab_copy(s // 2).wait()
        if s >= 1:
            if s % 2 == 1:
                turn_copy(s // 2).wait()
            if s >= 3:
                out_copy(s - 3).wait()
            out = outs[(s - 1) % 2]
            covered = (3 * (lon_ref[(s - 1) // 2] // 4)) // 128 + 11

            def clear(tile, _):
                out[:, pl.ds(pl.multiple_of(tile * 128, 128), 128)] = jnp.zeros((HALF, 128), F32)
                return 0

            lax.fori_loop(covered, 40, clear, 0)

        def block(n, _):
            if s < 4:
                product(s, pl.multiple_of(n * 256, 256), 256)
            if s >= 1:
                unit(s - 1, n * 2, parts0)
                unit(s - 1, jnp.minimum(n * 2 + 1, HALF // 8 - 1), parts1)
            return 0

        lax.fori_loop(0, 5, block, 0)
        if s < 4:

            @pl.when(lon_ref[s // 2] > 5120)
            def _():
                product(s, 1280, 128)

        if s >= 1:
            out_copy(s - 1).start()
    out_copy(2).wait()
    out_copy(3).wait()


def on_device(legendre, spectral, slot_wave, band_rows, lon_count):
    perm = jnp.asarray(placement_matrix(), BF16)
    anywhere = pl.BlockSpec(memory_space=pl.ANY)
    smem = pl.BlockSpec(memory_space=pltpu.SMEM)
    dma = pltpu.SemaphoreType.DMA
    n_gather = len(PLANE) + len(LINE)
    lhs, tab, turn = pl.pallas_call(
        exchange,
        out_shape=(
            jax.ShapeDtypeStruct((4, ROWS, 640), BF16),
            jax.ShapeDtypeStruct((2, 640, WIDTH), BF16),
            jax.ShapeDtypeStruct((2, TURNS, WIDTH), F32),
        ),
        in_specs=[smem, smem, smem, anywhere, anywhere, anywhere],
        out_specs=(anywhere, anywhere, anywhere),
        scratch_shapes=[
            pltpu.VMEM((SLOTS, DEPTH, NORTH), BF16),
            pltpu.VMEM((SLOTS, COLS, DEPTH), BF16),
            pltpu.VMEM((2, RE_ROWS, 1024), BF16),
            pltpu.VMEM((4, 160, DEPTH), BF16),
            pltpu.VMEM((SLOTS * COLS, 128), F32),
            pltpu.VMEM((SLOTS * COLS, 128), F32),
            pltpu.VMEM((PEERS, 1, 128), F32),
            pltpu.VMEM((SLOTS, 128), jnp.int32),
            pltpu.SMEM((SLOTS, 128), jnp.int32),
            pltpu.VMEM((2, PEERS, 256), BF16),
            pltpu.VMEM((len(GROUPS) * PEERS * PITCH, 128), F32),
            pltpu.VMEM((len(GROUPS) * PEERS * PITCH, 128), F32),
            pltpu.VMEM((2, 256, 1024), BF16),
            pltpu.VMEM((4, ROWS, 640), BF16),
            pltpu.VMEM((2, 640, WIDTH), BF16),
            pltpu.VMEM((2, TURNS, WIDTH), F32),
            dma((CHUNKS, 2)),
            dma,
            dma,
            dma((n_gather,)),
            dma((n_gather,)),
            dma((len(GROUPS),)),
            dma((len(GROUPS),)),
            dma((len(GROUPS),)),
            dma((CHUNKS,)),
            dma,
            dma,
        ],
        compiler_params=pltpu.CompilerParams(collective_id=0, has_side_effects=True, vmem_limit_bytes=58 << 20),
    )(band_rows, lon_count, slot_wave, legendre, jnp.swapaxes(spectral, 1, 2), perm)
    return pl.pallas_call(
        synthesis,
        out_shape=jax.ShapeDtypeStruct((2, FIELDS, LONS), F32),
        in_specs=[smem, anywhere, anywhere, anywhere],
        out_specs=anywhere,
        scratch_shapes=[
            pltpu.VMEM((4, ROWS, 640), BF16),
            pltpu.VMEM((2, 640, WIDTH), BF16),
            pltpu.VMEM((2, TURNS, WIDTH), F32),
            pltpu.VMEM((ROWS, WIDTH), F32),
            pltpu.VMEM((ROWS, WIDTH), F32),
            pltpu.VMEM((32, WIDTH), F32),
            pltpu.VMEM((32, WIDTH), F32),
            pltpu.VMEM((HALF, LONS), F32),
            pltpu.VMEM((HALF, LONS), F32),
            dma((4,)),
            dma((2,)),
            dma((2,)),
            dma((2,)),
        ],
        compiler_params=pltpu.CompilerParams(vmem_limit_bytes=58 << 20),
    )(lon_count, lhs, tab, turn)


def solution(mesh):
    return jax.shard_map(
        on_device,
        mesh=mesh,
        in_specs=(
            P("wave", None, None),
            P("wave", None, "lev"),
            P("wave"),
            P(("wave", "lev")),
            P(("wave", "lev")),
        ),
        out_specs=P(("wave", "lev"), None, None),
        check_vma=False,
    )
```

time: 85.1 us -> 71.2 us (0.84)
  Pallas kernels: 83.6 us -> 71 us
  other arithmetic: 1.29 us -> 0 us
    pallas_call x2, Pallas kernels: 83.6 us -> 71 us  [the longest x1 57.5 us: on_device(): pl.pallas_call(exchange, out_shape=(jax.ShapeDtypeStruct((4, ROWS, 640),...]
where the time goes in v2:
time: 71.2 us; the launch traced here: 71 us
  Pallas kernels  71 us (100%)
    pallas_call x1, Pallas kernels, on_device(): pl.pallas_call(exchange, out_shape=(jax.ShapeDtypeStruct((4, ROWS, 640),...  57.5 us
    pallas_call x1, Pallas kernels, on_device(): pl.pallas_call(synthesis, out_shape=jax.ShapeDtypeStruct((2, FIELDS, LONS...  13.5 us

profile of v2, /device:TPU:1, one launch (start us, length us, event | category | flops | bytes accessed | tf_op | source)
XLA Modules:
  0.0 71.0 jit_solution(17470211013308150681)
XLA Ops:
  0.0 57.5 %shard_map.64 = (bf16[4,504,640]{2,1,0:T(8,128)(2,1)}, bf16[2,640,1408]{2,1,0:T(8,128)(2,1)}, f32[2,56,1408]{2,1,0:T(8,128)}) custom-call(s32[2]{0:T(128)} %rows_ref.1, s32[2]{0:T(128)} %lon_ref.3, s32[40]{0:T(128)} %wave_ref.1, bf16[40,1280,128]{2,1,0:T(8,128)(2,1)} %leg_hbm.1, bf16[40,72,1280]{2,1,0:T(8,128)(2,1)} %bitcast.1, ...), custom_call_target="tpu_custom_call" | custom-call | tf_op jit(solution)/shard_map/pallas_call | solution.py:462
  57.5 13.5 %shard_map.65 = f32[2,144,5136]{2,1,0:T(8,128)} custom-call(s32[2]{0:T(128)} %lon_ref.3, bf16[4,504,640]{2,1,0:T(8,128)(2,1)} %get-tuple-element.8.lhs_hbm, bf16[2,640,1408]{2,1,0:T(8,128)(2,1)} %get-tuple-element.9.tab_hbm, f32[2,56,1408]{2,1,0:T(8,128)} %get-tuple-element.10.turn_hbm), custom_call_target="tpu_custom_call" | custom-call | tf_op jit(solution)/shard_map/pallas_call | solution.py:502

commit v3 on v2

--- a/solution.py
+++ b/solution.py
@@ -432,15 +432,11 @@
 
             lax.fori_loop(covered, 40, clear, 0)
 
-        def block(n, _):
-            if s < 4:
-                product(s, pl.multiple_of(n * 256, 256), 256)
-            if s >= 1:
-                unit(s - 1, n * 2, parts0)
-                unit(s - 1, jnp.minimum(n * 2 + 1, HALF // 8 - 1), parts1)
-            return 0
-
-        lax.fori_loop(0, 5, block, 0)
+        if s < 4:
+            product(s, 0, 1280)
+        if s >= 1:
+            for b in range(HALF // 8):
+                unit(s - 1, b, (parts0, parts1)[b % 2])
         if s < 4:
 
             @pl.when(lon_ref[s // 2] > 5120)

time: 71.2 us -> 68.2 us (0.958)
  Pallas kernels: 71 us -> 68 us
    pallas_call x1, Pallas kernels: 13.5 us -> 10.5 us  [on_device(): pl.pallas_call(synthesis, out_shape=jax.ShapeDtypeStruct((2, FIELDS, LONS...]
where the time goes in v3:
time: 68.2 us; the launch traced here: 68.1 us
  Pallas kernels  68 us (100%)
    pallas_call x1, Pallas kernels, on_device(): pl.pallas_call(exchange, out_shape=(jax.ShapeDtypeStruct((4, ROWS, 640),...  57.5 us
    pallas_call x1, Pallas kernels, on_device(): pl.pallas_call(synthesis, out_shape=jax.ShapeDtypeStruct((2, FIELDS, LONS...  10.5 us

profile of v3, /device:TPU:1, one launch (start us, length us, event | category | flops | bytes accessed | tf_op | source)
XLA Modules:
  0.0 68.1 jit_solution(6703389527541230783)
XLA Ops:
  0.0 57.5 %shard_map.64 = (bf16[4,504,640]{2,1,0:T(8,128)(2,1)}, bf16[2,640,1408]{2,1,0:T(8,128)(2,1)}, f32[2,56,1408]{2,1,0:T(8,128)}) custom-call(s32[2]{0:T(128)} %rows_ref.1, s32[2]{0:T(128)} %lon_ref.3, s32[40]{0:T(128)} %wave_ref.1, bf16[40,1280,128]{2,1,0:T(8,128)(2,1)} %leg_hbm.1, bf16[40,72,1280]{2,1,0:T(8,128)(2,1)} %bitcast.1, ...), custom_call_target="tpu_custom_call" | custom-call | tf_op jit(solution)/shard_map/pallas_call | solution.py:458
  57.5 10.5 %shard_map.65 = f32[2,144,5136]{2,1,0:T(8,128)} custom-call(s32[2]{0:T(128)} %lon_ref.3, bf16[4,504,640]{2,1,0:T(8,128)(2,1)} %get-tuple-element.8.lhs_hbm, bf16[2,640,1408]{2,1,0:T(8,128)(2,1)} %get-tuple-element.9.tab_hbm, f32[2,56,1408]{2,1,0:T(8,128)} %get-tuple-element.10.turn_hbm), custom_call_target="tpu_custom_call" | custom-call | tf_op jit(solution)/shard_map/pallas_call | solution.py:498

commit v4 on v3

--- a/solution.py
+++ b/solution.py
@@ -162,19 +162,19 @@
             )
         return copies
 
-    legendre_part(0)
-    legendre_part(1)
     pl.semaphore_wait(barrier, len(PLANE) + len(LINE))
     plane = gather(PLANE, 1, 0)
     for copy in plane:
         copy.start()
+    legendre_part(0)
+    legendre_part(1)
     legendre_part(2)
-    legendre_part(3)
     for copy in plane:
         copy.wait()
     line = gather(LINE, 16, len(PLANE))
     for copy in line:
         copy.start()
+    legendre_part(3)
     legendre_part(4)
     for copy in line:
         copy.wait()
@@ -352,9 +352,9 @@
     def turn_copy(r):
         return pltpu.make_async_copy(turn_hbm.at[r], turn.at[r], turn_sem.at[r])
 
-    def out_copy(s):
-        rows = out_hbm.at[s // 2, pl.ds((s % 2) * HALF, HALF), :]
-        return pltpu.make_async_copy(outs[s % 2], rows, out_sem.at[s % 2])
+    def out_copy(s, third):
+        rows = out_hbm.at[s // 2, pl.ds((s % 2) * HALF + third * 24, 24), :]
+        return pltpu.make_async_copy(outs[s % 2].at[pl.ds(third * 24, 24), :], rows, out_sem.at[s % 2, third])
 
     tab_copy(0).start()
     lhs_copy(0).start()
@@ -422,7 +422,8 @@
             if s % 2 == 1:
                 turn_copy(s // 2).wait()
             if s >= 3:
-                out_copy(s - 3).wait()
+                for third in range(3):
+                    out_copy(s - 3, third).wait()
             out = outs[(s - 1) % 2]
             covered = (3 * (lon_ref[(s - 1) // 2] // 4)) // 128 + 11
 
@@ -437,16 +438,17 @@
         if s >= 1:
             for b in range(HALF // 8):
                 unit(s - 1, b, (parts0, parts1)[b % 2])
+                if b % 3 == 2:
+                    out_copy(s - 1, b // 3).start()
         if s < 4:
 
             @pl.when(lon_ref[s // 2] > 5120)
             def _():
                 product(s, 1280, 128)
 
-        if s >= 1:
-            out_copy(s - 1).start()
-    out_copy(2).wait()
-    out_copy(3).wait()
+    for s in (2, 3):
+        for third in range(3):
+            out_copy(s, third).wait()
 
 
 def on_device(legendre, spectral, slot_wave, band_rows, lon_count):
@@ -513,7 +515,7 @@
             dma((4,)),
             dma((2,)),
             dma((2,)),
-            dma((2,)),
+            dma((2, 3)),
         ],
         compiler_params=pltpu.CompilerParams(vmem_limit_bytes=58 << 20),
     )(lon_count, lhs, tab, turn)

time: 68.2 us -> 67.4 us (0.988)
  Pallas kernels: 68 us -> 67.1 us
where the time goes in v4:
time: 67.4 us; the launch traced here: 67.3 us
  Pallas kernels  67.1 us (100%)
    pallas_call x1, Pallas kernels, on_device(): pl.pallas_call(exchange, out_shape=(jax.ShapeDtypeStruct((4, ROWS, 640),...  57.1 us
    pallas_call x1, Pallas kernels, on_device(): pl.pallas_call(synthesis, out_shape=jax.ShapeDtypeStruct((2, FIELDS, LONS...  10.1 us

profile of v4, /device:TPU:1, one launch (start us, length us, event | category | flops | bytes accessed | tf_op | source)
XLA Modules:
  0.0 67.3 jit_solution(3553872823463769091)
XLA Ops:
  0.0 57.1 %shard_map.64 = (bf16[4,504,640]{2,1,0:T(8,128)(2,1)}, bf16[2,640,1408]{2,1,0:T(8,128)(2,1)}, f32[2,56,1408]{2,1,0:T(8,128)}) custom-call(s32[2]{0:T(128)} %rows_ref.1, s32[2]{0:T(128)} %lon_ref.3, s32[40]{0:T(128)} %wave_ref.1, bf16[40,1280,128]{2,1,0:T(8,128)(2,1)} %leg_hbm.1, bf16[40,72,1280]{2,1,0:T(8,128)(2,1)} %bitcast.1, ...), custom_call_target="tpu_custom_call" | custom-call | tf_op jit(solution)/shard_map/pallas_call | solution.py:460
  57.1 10.1 %shard_map.65 = f32[2,144,5136]{2,1,0:T(8,128)} custom-call(s32[2]{0:T(128)} %lon_ref.3, bf16[4,504,640]{2,1,0:T(8,128)(2,1)} %get-tuple-element.8.lhs_hbm, bf16[2,640,1408]{2,1,0:T(8,128)(2,1)} %get-tuple-element.9.tab_hbm, f32[2,56,1408]{2,1,0:T(8,128)} %get-tuple-element.10.turn_hbm), custom_call_target="tpu_custom_call" | custom-call | tf_op jit(solution)/shard_map/pallas_call | solution.py:500
